TPU v7x, 32 devices: a whole 2x2x4 slice. The times are simulated.
32 devices in a mesh: dp: 16 (over z, y, core), blk: 2 (over x).
Axes of the slice: x: 2, y: 2, z: 4, core: 2. Of those that a mesh axis runs over, the one named last changes fastest.
Arguments:
- tokens: bfloat16 [16, 1024, 768], P('dp', 'blk'), may hold values from -6 to 6
- segments: int32 [16, 1024], P('dp'), may hold values from 0 to 15, never falling along the last dimension, each value on 1 to 198 neighbouring positions
- cotangent: bfloat16 [16, 1024, 768], P('dp', 'blk'), may hold values from -6 to 6
- qkv_weight: float32 [768, 2304], P(('dp', 'blk')), may hold values from -0.21875 to 0.21875
- proj_weight: float32 [768, 768], P(('dp', 'blk')), may hold values from -0.875 to 0.875
- up_weight: float32 [768, 3072], P(('dp', 'blk')), may hold values from -0.21875 to 0.21875
- down_weight: float32 [3072, 768], P(('dp', 'blk')), may hold values from -0.109375 to 0.109375
- vec_params: float32 [12, 768], P(None, ('dp', 'blk')), may hold values from -1.25 to 1.25
- qkv_velocity: float32 [768, 2304], P(('dp', 'blk')), may hold values from -80 to 80
- proj_velocity: float32 [768, 768], P(('dp', 'blk')), may hold values from -40 to 40
- up_velocity: float32 [768, 3072], P(('dp', 'blk')), may hold values from -40 to 40
- down_velocity: float32 [3072, 768], P(('dp', 'blk')), may hold values from -40 to 40
- vec_velocity: float32 [12, 768], P(None, ('dp', 'blk')), may hold values from -80 to 80
- qkv_average: float32 [768, 2304], P(('dp', 'blk')), may hold values from -0.109375 to 0.109375
- proj_average: float32 [768, 768], P(('dp', 'blk')), may hold values from -0.4375 to 0.4375
- up_average: float32 [768, 3072], P(('dp', 'blk')), may hold values from -0.109375 to 0.109375
- down_average: float32 [3072, 768], P(('dp', 'blk')), may hold values from -0.0546875 to 0.0546875
- vec_average: float32 [12, 768], P(None, ('dp', 'blk')), may hold values from -0.625 to 0.625
Outputs:
- output: bfloat16 [16, 1024, 768], P('dp', 'blk')
- tokens_grad: bfloat16 [16, 1024, 768], P('dp', 'blk')
- qkv_grad: float32 [768, 2304], P(('dp', 'blk'))
- proj_grad: float32 [768, 768], P(('dp', 'blk'))
- up_grad: float32 [768, 3072], P(('dp', 'blk'))
- down_grad: float32 [3072, 768], P(('dp', 'blk'))
- vec_grad: float32 [12, 768], P(None, ('dp', 'blk'))
- qkv_master: float32 [768, 2304], P(('dp', 'blk'))
- proj_master: float32 [768, 768], P(('dp', 'blk'))
- up_master: float32 [768, 3072], P(('dp', 'blk'))
- down_master: float32 [3072, 768], P(('dp', 'blk'))
- vec_master: float32 [12, 768], P(None, ('dp', 'blk'))
- qkv_velocity_out: float32 [768, 2304], P(('dp', 'blk'))
- proj_velocity_out: float32 [768, 768], P(('dp', 'blk'))
- up_velocity_out: float32 [768, 3072], P(('dp', 'blk'))
- down_velocity_out: float32 [3072, 768], P(('dp', 'blk'))
- vec_velocity_out: float32 [12, 768], P(None, ('dp', 'blk'))
- qkv_average_out: float32 [768, 2304], P(('dp', 'blk'))
- proj_average_out: float32 [768, 768], P(('dp', 'blk'))
- up_average_out: float32 [768, 3072], P(('dp', 'blk'))
- down_average_out: float32 [3072, 768], P(('dp', 'blk'))
- vec_average_out: float32 [12, 768], P(None, ('dp', 'blk'))
- qkv_copy: bfloat16 [768, 2304], P(('dp', 'blk'))
- proj_copy: bfloat16 [768, 768], P(('dp', 'blk'))
- up_copy: bfloat16 [768, 3072], P(('dp', 'blk'))
- down_copy: bfloat16 [3072, 768], P(('dp', 'blk'))
- vec_copy: bfloat16 [12, 768], P(None, ('dp', 'blk'))
Inputs may be any that keep to these rules, and one draw needn't show every extreme that they name: `segments`: in each row the ids never fall; each image holds 1 to 198 consecutive positions, and some image holds exactly 198; every id from 0 to the largest occurs.
All inputs are finite; a program needn't handle non-finite values.
Results may differ from a plain program's by a relative error of at most 0.014.
Values may be sent and summed in bfloat16 or wider, within the bound.
A program may use at most 256 MiB of HBM per device.

v0:
```python
import math

import jax
import jax.numpy as jnp
from jax import lax
from jax.sharding import PartitionSpec as P

D = 768
HEADS = 12
HEAD_DIM = 64


def layer_norm(value, gain, shift):
    mean = jnp.mean(value, axis=-1, keepdims=True)
    cent = value - mean
    var = jnp.mean(cent * cent, axis=-1, keepdims=True)
    return cent * lax.rsqrt(var + 1e-06) * (1.0 + gain) + shift


def gelu_exact(value):
    return jax.nn.gelu(value, approximate=False)


def contract_tokens(left, right):
    return lax.dot_general(
        left.reshape(-1, left.shape[-1]),
        right.reshape(-1, right.shape[-1]),
        (((0,), (0,)), ((), ())),
        preferred_element_type=jnp.float32,
    )


def times_transpose(left, weight):
    return lax.dot_general(
        left, weight, (((left.ndim - 1,), (1,)), ((), ())), preferred_element_type=jnp.float32
    )


def group_size(rows, block):
    limit = max(1, 512 // block)
    best = 1
    for cand in range(1, rows + 1):
        if rows % cand == 0 and cand <= limit:
            best = cand
    return best


def scores_of(query, keys, seg_query, seg_keys):
    scores = jnp.einsum(
        "gqhd,gkhd->ghqk", query, keys, preferred_element_type=jnp.float32
    ) * HEAD_DIM ** (-0.5)
    allowed = (seg_query[:, :, None] == seg_keys[:, None, :])[:, None]
    return (scores, allowed)


def attend_back(query, kv_all, grad_out, seg_query, segments, group):
    rows, block = (query.shape[0], query.shape[1])
    length = kv_all.shape[1]
    keys = kv_all[0:group, :, :D].reshape(group, length, HEADS, HEAD_DIM)
    values = kv_all[0:group, :, D:].reshape(group, length, HEADS, HEAD_DIM)
    scores, allowed = scores_of(query, keys, seg_query, segments)
    probs = jax.nn.softmax(jnp.where(allowed, scores, -1e30), axis=-1)
    probs_low = probs.astype(jnp.bfloat16)
    prob_grad = jnp.einsum("gqhd,gkhd->ghqk", grad_out, values, preferred_element_type=jnp.float32)
    score_grad = probs * (prob_grad - jnp.sum(probs * prob_grad, axis=-1, keepdims=True))
    score_low = score_grad.astype(jnp.bfloat16)
    dq_part = jnp.einsum(
        "ghqk,gkhd->gqhd", score_low, keys, preferred_element_type=jnp.float32
    ) * HEAD_DIM ** (-0.5)
    dk_part = jnp.einsum(
        "ghqk,gqhd->gkhd", score_low, query, preferred_element_type=jnp.float32
    ) * HEAD_DIM ** (-0.5)
    dv_part = jnp.einsum("ghqk,gqhd->gkhd", probs_low, grad_out, preferred_element_type=jnp.float32)
    dq_parts = dq_part.reshape(group, block, D)
    dkv_parts = jnp.concatenate(
        [dk_part.reshape(group, length, D), dv_part.reshape(group, length, D)], axis=-1
    )
    return (dq_parts, dkv_parts)


def update(weight, grad, velocity, average, rate):
    step_value = grad + 0.0005 * weight
    velocity_new = 0.9 * velocity + step_value
    weight_new = weight - rate * (step_value + 0.9 * velocity_new)
    average_new = 0.9 * average + 0.1 * weight_new
    return (weight_new, velocity_new, average_new)


def on_device(
    tokens,
    segments,
    cotangent,
    qkv_weight,
    proj_weight,
    up_weight,
    down_weight,
    vec_params,
    qkv_velocity,
    proj_velocity,
    up_velocity,
    down_velocity,
    vec_velocity,
    qkv_average,
    proj_average,
    up_average,
    down_average,
    vec_average,
):
    rows, block = (tokens.shape[0], tokens.shape[1])
    length = segments.shape[1]
    total_tokens = rows * lax.axis_size("dp") * length
    rate = 0.05 / math.sqrt(total_tokens)
    group = group_size(rows, block)
    gathered = (
        lax.all_gather(qkv_weight.astype(jnp.bfloat16), ("dp", "blk"), axis=0, tiled=True),
        lax.all_gather(proj_weight.astype(jnp.bfloat16), ("dp", "blk"), axis=0, tiled=True),
        lax.all_gather(up_weight.astype(jnp.bfloat16), ("dp", "blk"), axis=0, tiled=True),
        lax.all_gather(down_weight.astype(jnp.bfloat16), ("dp", "blk"), axis=0, tiled=True),
        lax.all_gather(vec_params.astype(jnp.bfloat16), ("dp", "blk"), axis=1, tiled=True),
    )
    w_query, w_proj, w_up, w_down, vec_low = gathered
    vec = vec_low.astype(jnp.float32)
    bias_up = vec[8:12].reshape(-1)
    position = lax.axis_index("blk")
    seg_query = lax.dynamic_slice_in_dim(segments, position * block, block, 1)
    inputs = tokens.astype(jnp.float32)
    a_one = layer_norm(inputs, vec[0], vec[1]).astype(jnp.bfloat16)
    zero_bias = jnp.zeros_like(vec[2])
    pre = jnp.dot(a_one, w_query, preferred_element_type=jnp.float32) + jnp.concatenate(
        [vec[2], zero_bias, vec[3]]
    )
    qkv = pre.astype(jnp.bfloat16)
    query = qkv[..., :D].reshape(rows, block, HEADS, HEAD_DIM)
    key_value = qkv[..., D:]
    piece = lax.all_gather(key_value, "blk", axis=1, tiled=True)
    top = jnp.full((rows, HEADS, block), -1e30, jnp.float32)
    count = piece.shape[1]
    keys = piece[0:group, :, :D].reshape(group, count, HEADS, HEAD_DIM)
    values = piece[0:group, :, D:].reshape(group, count, HEADS, HEAD_DIM)
    scores, allowed = scores_of(query, keys, seg_query, segments)
    scores = jnp.where(allowed, scores, -1e30)
    new_top = jnp.maximum(top, jnp.max(scores, axis=-1))
    weights = jnp.where(allowed, jnp.exp(scores - new_top[..., None]), 0.0)
    denoms = jnp.sum(weights, axis=-1)
    added = jnp.einsum(
        "ghqk,gkhd->gqhd", weights.astype(jnp.bfloat16), values, preferred_element_type=jnp.float32
    )
    mixed = (added / jnp.transpose(denoms, (0, 2, 1))[..., None]).reshape(rows, block, D)
    mixed_low = mixed.astype(jnp.bfloat16)
    second = inputs + jnp.dot(mixed_low, w_proj, preferred_element_type=jnp.float32) + vec[4]
    second_norm, norm_two_back = jax.vjp(layer_norm, second, vec[5], vec[6])
    a_two = second_norm.astype(jnp.bfloat16)
    hidden = jnp.dot(a_two, w_up, preferred_element_type=jnp.float32) + bias_up
    act_value, gelu_back = jax.vjp(gelu_exact, hidden)
    act = act_value.astype(jnp.bfloat16)
    result = second + jnp.dot(act, w_down, preferred_element_type=jnp.float32) + vec[7]
    output = result.astype(jnp.bfloat16)
    out_grad = cotangent.astype(jnp.float32)
    grad_down = contract_tokens(act, cotangent)
    bias_down_grad = jnp.sum(out_grad, axis=(0, 1))
    act_grad = times_transpose(cotangent, w_down)
    hidden_grad = gelu_back(act_grad)[0].astype(jnp.bfloat16)
    bias_up_grad = jnp.sum(hidden_grad.astype(jnp.float32), axis=(0, 1))
    grad_up = contract_tokens(a_two, hidden_grad)
    a_two_grad = times_transpose(hidden_grad, w_up)
    second_part, gain_two_grad, shift_two_grad = norm_two_back(a_two_grad)
    second_grad = out_grad + second_part
    attn_grad = second_grad.astype(jnp.bfloat16)
    bias_proj_grad = jnp.sum(attn_grad.astype(jnp.float32), axis=(0, 1))
    grad_proj = contract_tokens(mixed_low, attn_grad)
    mixed_grad = (
        times_transpose(attn_grad, w_proj)
        .astype(jnp.bfloat16)
        .reshape(rows, block, HEADS, HEAD_DIM)
    )
    kv_again = lax.all_gather(key_value, "blk", axis=1, tiled=True)
    query_grad, kv_terms = attend_back(query, kv_again, mixed_grad, seg_query, segments, group)
    kv_grad = lax.psum_scatter(
        kv_terms.astype(jnp.bfloat16), "blk", scatter_dimension=1, tiled=True
    ).astype(jnp.float32)
    qkv_grad_low = jnp.concatenate([query_grad, kv_grad], axis=-1).astype(jnp.bfloat16)
    qkv_sums = jnp.sum(qkv_grad_low.astype(jnp.float32), axis=(0, 1))
    grad_query = contract_tokens(a_one, qkv_grad_low)
    a_one_grad = times_transpose(qkv_grad_low, w_query)
    norm_one_back = jax.vjp(layer_norm, inputs, vec[0], vec[1])[1]
    first_part, gain_one_grad, shift_one_grad = norm_one_back(a_one_grad)
    tokens_grad = (second_grad + first_part).astype(jnp.bfloat16)
    vec_local = jnp.concatenate(
        [
            jnp.stack(
                [
                    gain_one_grad,
                    shift_one_grad,
                    qkv_sums[:D],
                    qkv_sums[2 * D :],
                    bias_proj_grad,
                    gain_two_grad,
                    shift_two_grad,
                    bias_down_grad,
                ]
            ),
            bias_up_grad.reshape(4, D),
        ],
        axis=0,
    )
    query_share, proj_share, up_share, down_share, vec_share = (
        lax.psum_scatter(grad_query, ("dp", "blk"), scatter_dimension=0, tiled=True),
        lax.psum_scatter(grad_proj, ("dp", "blk"), scatter_dimension=0, tiled=True),
        lax.psum_scatter(grad_up, ("dp", "blk"), scatter_dimension=0, tiled=True),
        lax.psum_scatter(grad_down, ("dp", "blk"), scatter_dimension=0, tiled=True),
        lax.psum_scatter(vec_local, ("dp", "blk"), scatter_dimension=1, tiled=True),
    )
    qkv_new = update(qkv_weight, query_share, qkv_velocity, qkv_average, rate)
    proj_new = update(proj_weight, proj_share, proj_velocity, proj_average, rate)
    up_new = update(up_weight, up_share, up_velocity, up_average, rate)
    down_new = update(down_weight, down_share, down_velocity, down_average, rate)
    vec_new = update(vec_params, vec_share, vec_velocity, vec_average, rate)
    return (
        output,
        tokens_grad,
        query_share,
        proj_share,
        up_share,
        down_share,
        vec_share,
        qkv_new[0],
        proj_new[0],
        up_new[0],
        down_new[0],
        vec_new[0],
        qkv_new[1],
        proj_new[1],
        up_new[1],
        down_new[1],
        vec_new[1],
        qkv_new[2],
        proj_new[2],
        up_new[2],
        down_new[2],
        vec_new[2],
        qkv_new[0].astype(jnp.bfloat16),
        proj_new[0].astype(jnp.bfloat16),
        up_new[0].astype(jnp.bfloat16),
        down_new[0].astype(jnp.bfloat16),
        vec_new[0].astype(jnp.bfloat16),
    )


def solution(mesh):
    return jax.shard_map(
        on_device,
        mesh=mesh,
        in_specs=(
            P("dp", "blk", None),
            P("dp", None),
            P("dp", "blk", None),
            P(("dp", "blk"), None),
            P(("dp", "blk"), None),
            P(("dp", "blk"), None),
            P(("dp", "blk"), None),
            P(None, ("dp", "blk")),
            P(("dp", "blk"), None),
            P(("dp", "blk"), None),
            P(("dp", "blk"), None),
            P(("dp", "blk"), None),
            P(None, ("dp", "blk")),
            P(("dp", "blk"), None),
            P(("dp", "blk"), None),
            P(("dp", "blk"), None),
            P(("dp", "blk"), None),
            P(None, ("dp", "blk")),
        ),
        out_specs=(
            P("dp", "blk", None),
            P("dp", "blk", None),
            P(("dp", "blk"), None),
            P(("dp", "blk"), None),
            P(("dp", "blk"), None),
            P(("dp", "blk"), None),
            P(None, ("dp", "blk")),
            P(("dp", "blk"), None),
            P(("dp", "blk"), None),
            P(("dp", "blk"), None),
            P(("dp", "blk"), None),
            P(None, ("dp", "blk")),
            P(("dp", "blk"), None),
            P(("dp", "blk"), None),
            P(("dp", "blk"), None),
            P(("dp", "blk"), None),
            P(None, ("dp", "blk")),
            P(("dp", "blk"), None),
            P(("dp", "blk"), None),
            P(("dp", "blk"), None),
            P(("dp", "blk"), None),
            P(None, ("dp", "blk")),
            P(("dp", "blk"), None),
            P(("dp", "blk"), None),
            P(("dp", "blk"), None),
            P(("dp", "blk"), None),
            P(None, ("dp", "blk")),
        ),
        check_vma=False,
    )
```

profile of v0, /device:TPU:0, one launch (start us, length us, event | category | flops | bytes accessed | tf_op | source)
XLA Modules:
  0.0 987.8 jit_solution(302901542613035314)
XLA Ops:
  9.6 70.8 %all-gather = bf16[32,24,12]{1,2,0:T(8,128)(2,1)S(1)} all-gather(bf16[1,24,12]{1,2,0:T(8,128)(2,1)S(1)} %convert_bitcast_fusion), channel_id=1, replica_groups=mesh['dp'=16,'blk'=2] {'dp','blk'}, dimensions={0}, use_global_device_ids=true | all-gather | bytes 19008 | tf_op jit(solution)/shard_map/all_gather | solution.py:119
  95.8 37.2 %all-gather.9.cloned.1.call-done = bf16[1,1024,1536]{2,1,0:T(8,128)(2,1)} async-done(((bf16[1,512,1536]{2,1,0:T(8,128)(2,1)}), bf16[1,1024,1536]{2,1,0:T(8,128)(2,1)}) %all-gather.9.cloned.1.call-update) | async-done | bytes 3145744 | tf_op jit(solution)/shard_map/all_gather | solution.py:135
  141.7 10.5 %fusion.4 = (f32[12,512]{1,0:T(8,128)S(1)}, f32[12,512,1024]{2,1,0:T(8,128)}) fusion(pred[512,1024]{1,0:T(8,128)(4,1)S(1)} %broadcast_compare_fusion, bf16[512,12,64]{0,2,1:T(8,128)(2,1)S(1)} %bitcast.126, bf16[1024,12,64]{0,2,1:T(8,128)(2,1)S(1)} %bitcast.124), kind=kOutput, calls=%fused_computation.9 | convolution fusion | flops 824174592 | bytes 28073984 | tf_op jit(solution)/shard_map/gqhd,gkhd->ghqk/dot_general | solution.py:49
  152.2 15.9 %fusion.1 = (f32[12,512]{1,0:T(8,128)S(1)}, f32[12,512]{1,0:T(8,128)S(1)}) fusion(f32[12,512,1024]{2,1,0:T(8,128)} %get-tuple-element.71, f32[12,512]{1,0:T(8,128)S(1)} %get-tuple-element.70, pred[512,1024]{1,0:T(8,128)(4,1)S(1)} %broadcast_compare_fusion, f32[12,512]{1,0:T(8,128)S(1)} %broadcast_maximum_fusion), kind=kLoop, calls=%fused_computation.6 | loop fusion | flops 44027904 | bytes 25788416 | tf_op jit(solution)/shard_map/reduce_sum | solution.py:62
  168.1 12.1 %fusion.33 = bf16[1,512,12,64]{1,3,2,0:T(8,128)(2,1)} fusion(bf16[1024,12,64]{0,2,1:T(8,128)(2,1)S(1)} %bitcast.135, f32[12,512,1024]{2,1,0:T(8,128)} %get-tuple-element.71, f32[12,512]{1,0:T(8,128)S(1)} %broadcast_maximum_fusion, pred[512,1024]{1,0:T(8,128)(4,1)S(1)} %broadcast_compare_fusion, f32[512,12]{0,1:T(8,128)S(1)} %bitcast.143), kind=kOutput, calls=%fused_computation.60 | convolution fusion | flops 837550080 | bytes 28098560 | tf_op jit(solution)/shard_map/ghqk,gkhd->gqhd/dot_general | solution.py:145
  180.2 10.5 %all-gather.11.cloned.1.call-done = bf16[768,768]{1,0:T(8,128)(2,1)} async-done(((bf16[24,768]{1,0:T(8,128)(2,1)}), bf16[768,768]{1,0:T(8,128)(2,1)}) %all-gather.11.cloned.1.call-update) | async-done | bytes 1179664 | tf_op jit(solution)/shard_map/all_gather | solution.py:116
  193.5 63.2 %all-gather.13.cloned.1.call-done = bf16[768,3072]{1,0:T(8,128)(2,1)} async-done(((bf16[24,3072]{1,0:T(8,128)(2,1)}), bf16[768,3072]{1,0:T(8,128)(2,1)}) %all-gather.13.cloned.1.call-update) | async-done | bytes 4718608 | tf_op jit(solution)/shard_map/all_gather | solution.py:117
  256.7 19.9 %multiply_convert_fusion.1 = (bf16[512,3072]{1,0:T(8,128)(2,1)S(1)}, f32[512,3072]{1,0:T(8,128)}, f32[512,3072]{1,0:T(8,128)}) fusion(f32[3072]{0:T(1024)S(1)} %add.210, bf16[768,3072]{1,0:T(8,128)(2,1)} %all-gather.13.cloned.1.call-done, f32[1,512,768]{2,1,0:T(8,128)S(1)} %get-tuple-element.73, f32[768]{0:T(1024)S(1)} %get-tuple-element.34, ...), kind=kOutput, calls=%fused_computation.18 | convolution fusion | flops 2521694208 | bytes 22042624 | tf_op jit(solution)/shard_map/dot_general | solution.py:153
  283.3 134.4 %reduce-scatter.15.cloned.1.call-done = f32[96,768]{1,0:T(8,128)} async-done(((f32[3072,768]{1,0:T(8,128)}), f32[96,768]{1,0:T(8,128)}) %reduce-scatter.15.cloned.1.call-update) | async-done | bytes 294928 | tf_op jit(solution)/shard_map/reduce_scatter | solution.py:210
  419.9 64.3 %all-gather.15.cloned.1.call-done = bf16[3072,768]{1,0:T(8,128)(2,1)} async-done(((bf16[96,768]{1,0:T(8,128)(2,1)}), bf16[3072,768]{1,0:T(8,128)(2,1)}) %all-gather.15.cloned.1.call-update) | async-done | bytes 4718608 | tf_op jit(solution)/shard_map/all_gather | solution.py:118
  484.2 8.4 convert_reduce_fusion
  492.7 6.4 fusion.34
  506.7 12.9 %fusion.24 = bf16[12,64,1024]{2,1,0:T(8,128)(2,1)} fusion(bf16[512,12,64]{0,2,1:T(8,128)(2,1)S(1)} %bitcast.137, f32[12,512,1024]{2,1,0:T(8,128)} %get-tuple-element.71, f32[12,512]{1,0:T(8,128)S(1)} %get-tuple-element.27, f32[12,512]{1,0:T(8,128)S(1)} %get-tuple-element.70, pred[512,1024]{1,0:T(8,128)(4,1)S(1)} %broadcast_compare_fusion), kind=kOutput, calls=%fused_computation.52 | convolution fusion | flops 837550080 | bytes 28098560 | tf_op jit(solution)/shard_map/ghqk,gqhd->gkhd/dot_general | solution.py:73
  519.6 21.0 %multiply_reduce_fusion = (f32[12,512]{1,0:T(8,128)S(1)}, f32[12,512,1024]{2,1,0:T(8,128)}) fusion(f32[12,512]{1,0:T(8,128)S(1)} %get-tuple-element.27, f32[12,512]{1,0:T(8,128)S(1)} %get-tuple-element.70, f32[12,512,1024]{2,1,0:T(8,128)} %get-tuple-element.71, pred[512,1024]{1,0:T(8,128)(4,1)S(1)} %broadcast_compare_fusion, ...), kind=kOutput, calls=%fused_computation.1 | convolution fusion | flops 843048960 | bytes 53288960 | tf_op jit(solution)/shard_map/gqhd,gkhd->ghqk/dot_general | solution.py:64
  540.6 17.4 %multiply_convert_fusion = bf16[12,512,1024]{2,1,0:T(8,128)(2,1)S(1)} fusion(f32[12,512,1024]{2,1,0:T(8,128)} %get-tuple-element.77, f32[12,512]{1,0:T(8,128)S(1)} %get-tuple-element.76, f32[12,512]{1,0:T(8,128)S(1)} %get-tuple-element.27, f32[12,512]{1,0:T(8,128)S(1)} %get-tuple-element.70, f32[12,512,1024]{2,1,0:T(8,128)} %get-tuple-element.71, ...), kind=kLoop, calls=%fused_computation | loop fusion | flops 44040192 | bytes 63512576 | tf_op jit(solution)/shard_map/convert_element_type | solution.py:66
  568.5 8.1 fusion.66
  577.9 9.5 multiply_convert_fusion.3
  587.5 19.5 %reduce-scatter.7.cloned.1.call-done = bf16[1,512,1536]{1,2,0:T(8,128)(2,1)} async-done(((bf16[1,1024,1536]{1,2,0:T(8,128)(2,1)}), bf16[1,512,1536]{1,2,0:T(8,128)(2,1)}) %reduce-scatter.7.cloned.1.call-update) | async-done | bytes 1572880 | tf_op jit(solution)/shard_map/reduce_scatter | solution.py:178
  607.0 7.1 fusion.38
  617.6 6.9 fusion.37
  624.5 87.4 %reduce-scatter.11.cloned.1.call-done = f32[24,768]{1,0:T(8,128)} async-done(((f32[768,768]{1,0:T(8,128)}), f32[24,768]{1,0:T(8,128)}) %reduce-scatter.11.cloned.1.call-update) | async-done | bytes 73744 | tf_op jit(solution)/shard_map/reduce_scatter | solution.py:208
  725.2 40.5 %all-reduce = f32[12,768]{1,0:T(8,128)S(1)} all-reduce(f32[12,768]{1,0:T(8,128)S(1)} %concatenate.55), channel_id=7, replica_groups=mesh['dp'=16,'blk'=2] {'dp','blk'}, use_global_device_ids=true, to_apply=%region_25.26.clone | all-reduce | flops 9216 | bytes 73728
  767.0 86.9 %reduce-scatter.13.cloned.1.call-done = f32[24,3072]{1,0:T(8,128)} async-done(((f32[768,3072]{1,0:T(8,128)}), f32[24,3072]{1,0:T(8,128)}) %reduce-scatter.13.cloned.1.call-update) | async-done | bytes 294928 | tf_op jit(solution)/shard_map/reduce_scatter | solution.py:209
  857.6 120.6 %reduce-scatter.9.cloned.1.call-done = f32[24,2304]{1,0:T(8,128)} async-done(((f32[768,2304]{1,0:T(8,128)}), f32[24,2304]{1,0:T(8,128)}) %reduce-scatter.9.cloned.1.call-update) | async-done | bytes 221200 | tf_op jit(solution)/shard_map/reduce_scatter | solution.py:207
  (190 shorter events, 81.4 us)
Async XLA Ops:
  7.2 77.1 %all-gather.7.cloned.1.call-start = ((), (), s32[]{:S(2)}) async-start(), calls=%async_computation.5 | async-start | bytes 3649536 | tf_op jit(solution)/shard_map/all_gather | solution.py:115
  8.9 124.1 %all-gather.9.cloned.1.call-start = ((), (), s32[]{:S(2)}) async-start(), calls=%async_computation.6 | async-start | bytes 4718592 | tf_op jit(solution)/shard_map/all_gather | solution.py:135
  92.1 98.7 %all-gather.11.cloned.1.call-start = ((), (), s32[]{:S(2)}) async-start(), calls=%async_computation.7 | async-start | bytes 1216512 | tf_op jit(solution)/shard_map/all_gather | solution.py:116
  92.8 163.9 %all-gather.13.cloned.1.call-start = ((), (), s32[]{:S(2)}) async-start(), calls=%async_computation.8 | async-start | bytes 4866048 | tf_op jit(solution)/shard_map/all_gather | solution.py:117
  93.6 324.2 %reduce-scatter.15.cloned.1.call-start = ((), (), s32[]{:S(2)}) async-start(), calls=%async_computation.14 | async-start | bytes 9732096 | tf_op jit(solution)/shard_map/reduce_scatter | solution.py:210
  193.2 299.5 %copy-start.6 = (f32[1,512,768]{2,1,0:T(8,128)}, f32[1,512,768]{2,1,0:T(8,128)S(1)}, u32[]{:S(2)}) copy-start(f32[1,512,768]{2,1,0:T(8,128)S(1)} %get-tuple-element.73) | copy-start | bytes 4718596
  283.2 201.0 %all-gather.15.cloned.1.call-start = ((), (), s32[]{:S(2)}) async-start(), calls=%async_computation.9 | async-start | bytes 4866048 | tf_op jit(solution)/shard_map/all_gather | solution.py:118
  419.8 194.3 %copy-start.18 = (f32[96,768]{1,0:T(8,128)}, f32[96,768]{1,0:T(8,128)S(1)}, u32[]{:S(2)}) copy-start(f32[96,768]{1,0:T(8,128)S(1)} %get-tuple-element.46) | copy-start | bytes 884740
  419.9 187.1 %reduce-scatter.7.cloned.1.call-start = ((), (), s32[]{:S(2)}) async-start(), calls=%async_computation.10 | async-start | bytes 4718592 | tf_op jit(solution)/shard_map/reduce_scatter | solution.py:178
  564.7 147.2 %reduce-scatter.11.cloned.1.call-start = ((), (), s32[]{:S(2)}) async-start(), calls=%async_computation.12 | async-start | bytes 2433024 | tf_op jit(solution)/shard_map/reduce_scatter | solution.py:208
  568.4 285.5 %reduce-scatter.13.cloned.1.call-start = ((), (), s32[]{:S(2)}) async-start(), calls=%async_computation.13 | async-start | bytes 9732096 | tf_op jit(solution)/shard_map/reduce_scatter | solution.py:209
  576.6 401.6 %reduce-scatter.9.cloned.1.call-start = ((), (), s32[]{:S(2)}) async-start(), calls=%async_computation.11 | async-start | bytes 7299072 | tf_op jit(solution)/shard_map/reduce_scatter | solution.py:207
  617.5 94.4 %copy-start.26 = (f32[24,768]{1,0:T(8,128)S(1)}, f32[24,768]{1,0:T(8,128)}, u32[]{:S(2)}) copy-start(f32[24,768]{1,0:T(8,128)} %param.22) | copy-start | bytes 221188
  617.5 94.3 %copy-start.29 = (f32[24,768]{1,0:T(8,128)S(1)}, f32[24,768]{1,0:T(8,128)}, u32[]{:S(2)}) copy-start(f32[24,768]{1,0:T(8,128)} %param.27) | copy-start | bytes 221188
  617.6 95.9 %copy-start.30 = (f32[24,768]{1,0:T(8,128)S(1)}, f32[24,768]{1,0:T(8,128)}, u32[]{:S(2)}) copy-start(f32[24,768]{1,0:T(8,128)} %param.32) | copy-start | bytes 221188
  719.4 46.3 %copy-start.38 = (f32[12,24]{1,0:T(8,128)S(1)}, f32[12,24]{1,0:T(8,128)}, u32[]{:S(2)}) copy-start(f32[12,24]{1,0:T(8,128)} %param.25) | copy-start | bytes 3460
  719.4 46.3 %copy-start.43 = (f32[12,24]{1,0:T(8,128)S(1)}, f32[12,24]{1,0:T(8,128)}, u32[]{:S(2)}) copy-start(f32[12,24]{1,0:T(8,128)} %param.30) | copy-start | bytes 3460
  719.5 46.9 %copy-start.42 = (f32[12,24]{1,0:T(8,128)S(1)}, f32[12,24]{1,0:T(8,128)}, u32[]{:S(2)}) copy-start(f32[12,24]{1,0:T(8,128)} %param.35) | copy-start | bytes 3460
  719.5 134.4 %copy-start.21 = (f32[24,3072]{1,0:T(8,128)S(1)}, f32[24,3072]{1,0:T(8,128)}, u32[]{:S(2)}) copy-start(f32[24,3072]{1,0:T(8,128)} %param.23) | copy-start | bytes 884740
  724.7 253.6 %copy-start.22 = (f32[24,2304]{1,0:T(8,128)S(1)}, f32[24,2304]{1,0:T(8,128)}, u32[]{:S(2)}) copy-start(f32[24,2304]{1,0:T(8,128)} %param.21) | copy-start | bytes 663556
  724.7 253.6 %copy-start.27 = (f32[24,2304]{1,0:T(8,128)S(1)}, f32[24,2304]{1,0:T(8,128)}, u32[]{:S(2)}) copy-start(f32[24,2304]{1,0:T(8,128)} %param.26) | copy-start | bytes 663556
  724.7 255.3 %copy-start.28 = (f32[24,2304]{1,0:T(8,128)S(1)}, f32[24,2304]{1,0:T(8,128)}, u32[]{:S(2)}) copy-start(f32[24,2304]{1,0:T(8,128)} %param.31) | copy-start | bytes 663556
  766.4 214.4 %copy-start.37 = (f32[12,24]{1,0:T(8,128)}, f32[12,24]{1,0:T(8,128)S(1)}, u32[]{:S(2)}) copy-start(f32[12,24]{1,0:T(8,128)S(1)} %get-tuple-element.42) | copy-start | bytes 3460
  855.8 124.9 %copy-start.19 = (f32[24,3072]{1,0:T(8,128)}, f32[24,3072]{1,0:T(8,128)S(1)}, u32[]{:S(2)}) copy-start(f32[24,3072]{1,0:T(8,128)S(1)} %get-tuple-element.49) | copy-start | bytes 884740
  (36 other events, 337.0 us)
Sparse Core Ops, SparseCore 0:
  11.5 63.2 all-gather.6
  92.2 40.7 all-gather.8
  136.5 54.1 all-gather.10
  194.1 62.5 all-gather.12
  283.3 134.3 reduce-scatter.14
  421.5 62.7 all-gather.14
  564.8 42.1 reduce-scatter.6
  612.8 99.0 reduce-scatter.10
  719.4 134.4 reduce-scatter.12
  860.0 118.2 reduce-scatter.8
where the time goes:
time: 992 us; the launch traced here: 988 us
  waiting for transfers between devices  624 us (63%)
  matrix products  148 us (15%)
  blocking collectives  111 us (11%)
  other arithmetic  66.1 us (7%)
  local copies, waits for them, and re-layouts  23 us (2%)
  between operations  15.1 us (2%)
    reduce_scatter x1, waiting for transfers between devices, on_device(): lax.psum_scatter(grad_down, ('dp', 'blk'), scatter_dimension=0, tiled=True)  134 us
    reduce_scatter x1, waiting for transfers between devices, on_device(): lax.psum_scatter(grad_query, ('dp', 'blk'), scatter_dimension=0, tiled=True)  121 us
    reduce_scatter x1, waiting for transfers between devices, on_device(): lax.psum_scatter(grad_proj, ('dp', 'blk'), scatter_dimension=0, tiled=True)  87.4 us
    reduce_scatter x1, waiting for transfers between devices, on_device(): lax.psum_scatter(grad_up, ('dp', 'blk'), scatter_dimension=0, tiled=True)  86.9 us
    all_gather x1, blocking collectives, on_device(): lax.all_gather(vec_params.astype(jnp.bfloat16), ('dp', 'blk'), axis=1, ti...  70.8 us
    all_gather x1, waiting for transfers between devices, on_device(): lax.all_gather(down_weight.astype(jnp.bfloat16), ('dp', 'blk'), axis=0, t...  64.3 us
    all_gather x1, waiting for transfers between devices, on_device(): lax.all_gather(up_weight.astype(jnp.bfloat16), ('dp', 'blk'), axis=0, til...  63.2 us
    unnamed x1, blocking collectives  40.5 us
  transfers between devices with their start and end apart: 10, of which 9 were waited for; matrix products, arithmetic and copies ran while one was open for 12% of the time, Pallas kernels for 0%

commit v1 on v0

--- a/solution.py
+++ b/solution.py
@@ -3,6 +3,8 @@
 import jax
 import jax.numpy as jnp
 from jax import lax
+from jax.experimental import pallas as pl
+from jax.experimental.pallas import tpu as pltpu
 from jax.sharding import PartitionSpec as P
 
 D = 768
@@ -246,9 +248,546 @@
     )
 
 
+PIECE = (48, 384)
+NP = 12
+Z, Y, X, C = 4, 2, 2, 2
+MESH = pl.DeviceIdType.MESH
+
+
+def place():
+    d, x = lax.axis_index("dp"), lax.axis_index("blk")
+    return d // (2 * Y), (d // 2) % Y, d % 2, x
+
+
+def ident(z, y, c, x):
+    return ((z * Y + y) * 2 + c, x)
+
+
+def greet(z, y, c, x):
+    barrier = pltpu.get_barrier_semaphore()
+    peers = [ident((z + k) % Z, y, c, x) for k in range(1, Z)]
+    peers += [ident(z, 1 - y, c, x), ident(z, y, c, 1 - x), ident(z, y, 1 - c, x)]
+    for peer in peers:
+        pl.semaphore_signal(barrier, inc=1, device_id=peer, device_id_type=MESH)
+    pl.semaphore_wait(barrier, len(peers))
+
+
+def remote(src, dst, send, recv, peer):
+    return pltpu.make_async_remote_copy(
+        src_ref=src, dst_ref=dst, send_sem=send, recv_sem=recv, device_id=peer, device_id_type=MESH
+    )
+
+
+def vec_steps(z, y, c, x):
+    return [
+        [ident(z, y, 1 - c, x)],
+        [ident(z, y, c, 1 - x)],
+        [ident(z, 1 - y, c, x)],
+        [ident((z + k) % Z, y, c, x) for k in range(1, Z)],
+    ]
+
+
+def vec_copies(step, now, got, send, recv, at):
+    peers = vec_steps(*at)[step]
+    return [
+        remote(now.at[step], got.at[step + k], send.at[step + k], recv.at[step + k], peer)
+        for k, peer in enumerate(peers)
+    ]
+
+
+def gather_kernel(unit, vec_in, full, vec_out, vec_now, vec_got, own_sem, send, recv, vsend, vrecv):
+    z, y, c, x = at = place()
+    own = pltpu.make_async_copy(unit, full.at[c, y, x, z], own_sem)
+    own.start()
+    vec_now[0] = vec_in[...]
+    greet(*at)
+
+    def first(t):
+        return [
+            remote(unit.at[t], full.at[c, y, x, z, t], send.at[t, k - 1], recv.at[t, k - 1], ident((z + k) % Z, y, c, x))
+            for k in range(1, Z)
+        ]
+
+    def second(t):
+        low, high = full.at[c, y, x, 0:2, t], full.at[c, y, x, 2:4, t]
+        return [
+            remote(low, low, send.at[t, 3], recv.at[t, 3], ident(z, y, c, 1 - x)),
+            remote(high, high, send.at[t, 4], recv.at[t, 4], ident(z, 1 - y, c, x)),
+        ]
+
+    def third(t):
+        low, high = full.at[c, y, :, 0:2, t], full.at[c, :, x, 2:4, t]
+        return [
+            remote(low, low, send.at[t, 5], recv.at[t, 5], ident(z, 1 - y, c, x)),
+            remote(high, high, send.at[t, 6], recv.at[t, 6], ident(z, y, c, 1 - x)),
+        ]
+
+    def last(t):
+        block = full.at[c, :, :, :, t]
+        return [remote(block, block, send.at[t, 7], recv.at[t, 7], ident(z, y, 1 - c, x))]
+
+    def begin(copies):
+        for copy in copies:
+            copy.start()
+
+    def arrive(copies):
+        for copy in copies:
+            copy.wait_recv()
+
+    for step in range(4):
+        copies = vec_copies(step, vec_now, vec_got, vsend, vrecv, at)
+        begin(copies)
+        if step < AHEAD:
+            begin(first(step))
+        arrive(copies)
+        total = vec_now[step]
+        for k in range(len(copies)):
+            total = total + vec_got[step + k]
+        if step < 3:
+            vec_now[step + 1] = total
+        else:
+            vec_out[...] = total
+    own.wait()
+
+    def body(i, _):
+        @pl.when(i + AHEAD < NP)
+        def _():
+            begin(first(i + AHEAD))
+
+        @pl.when(i < NP)
+        def _():
+            arrive(first(i))
+            begin(second(i))
+
+        @pl.when(jnp.logical_and(i >= 1, i < NP + 1))
+        def _():
+            arrive(second(i - 1))
+            begin(third(i - 1))
+
+        @pl.when(jnp.logical_and(i >= 2, i < NP + 2))
+        def _():
+            arrive(third(i - 2))
+            begin(last(i - 2))
+
+        return 0
+
+    lax.fori_loop(0, NP + 2, body, 0)
+
+    def done(t, _):
+        arrive(last(t))
+        for copy in first(t) + second(t) + third(t) + last(t):
+            copy.wait_send()
+        return 0
+
+    lax.fori_loop(0, NP, done, 0)
+    for step in range(4):
+        for copy in vec_copies(step, vec_now, vec_got, vsend, vrecv, at):
+            copy.wait_send()
+
+
+AHEAD = 3
+
+
+def gather_all(unit, vec_placed):
+    return pl.pallas_call(
+        gather_kernel,
+        out_shape=(
+            jax.ShapeDtypeStruct((C, Y, X, Z, NP) + PIECE, jnp.bfloat16),
+            jax.ShapeDtypeStruct(vec_placed.shape, jnp.bfloat16),
+        ),
+        in_specs=[pl.BlockSpec(memory_space=pl.ANY), pl.BlockSpec(memory_space=pltpu.VMEM)],
+        out_specs=(pl.BlockSpec(memory_space=pl.ANY), pl.BlockSpec(memory_space=pltpu.VMEM)),
+        scratch_shapes=[
+            pltpu.VMEM((4,) + vec_placed.shape, jnp.bfloat16),
+            pltpu.VMEM((6,) + vec_placed.shape, jnp.bfloat16),
+            pltpu.SemaphoreType.DMA,
+            pltpu.SemaphoreType.DMA((NP, 8)),
+            pltpu.SemaphoreType.DMA((NP, 8)),
+            pltpu.SemaphoreType.DMA((6,)),
+            pltpu.SemaphoreType.DMA((6,)),
+        ],
+        compiler_params=pltpu.CompilerParams(
+            collective_id=0, has_side_effects=True, vmem_limit_bytes=56 << 20
+        ),
+        name="gather_all",
+    )(unit, vec_placed)
+
+
+def scatter_kernel(
+    local_in, vec_in, out, vec_out, local, got_core, got_two, got_one, got_z, vec_now, vec_got, own_sem, send, recv, vsend, vrecv
+):
+    z, y, c, x = at = place()
+    own = pltpu.make_async_copy(local_in, local, own_sem)
+    own.start()
+    vec_now[0] = vec_in[...]
+    greet(*at)
+
+    def core(t):
+        return [
+            remote(local.at[1 - c, :, :, :, t], got_core.at[t], send.at[t, 0], recv.at[t, 0], ident(z, y, 1 - c, x))
+        ]
+
+    def two(t):
+        return [
+            remote(local.at[c, 1 - y, :, 0:2, t], got_two.at[t, 0], send.at[t, 1], recv.at[t, 1], ident(z, 1 - y, c, x)),
+            remote(local.at[c, :, 1 - x, 2:4, t], got_two.at[t, 1], send.at[t, 2], recv.at[t, 2], ident(z, y, c, 1 - x)),
+        ]
+
+    def one(t):
+        return [
+            remote(local.at[c, y, 1 - x, 0:2, t], got_one.at[t, 0], send.at[t, 3], recv.at[t, 3], ident(z, y, c, 1 - x)),
+            remote(local.at[c, 1 - y, x, 2:4, t], got_one.at[t, 1], send.at[t, 4], recv.at[t, 4], ident(z, 1 - y, c, x)),
+        ]
+
+    def along(t):
+        return [
+            remote(local.at[c, y, x, (z + k) % Z, t], got_z.at[t, k - 1], send.at[t, 4 + k], recv.at[t, 4 + k], ident((z + k) % Z, y, c, x))
+            for k in range(1, Z)
+        ]
+
+    def begin(copies):
+        for copy in copies:
+            copy.start()
+
+    def arrive(copies):
+        for copy in copies:
+            copy.wait_recv()
+
+    def add(a, b):
+        return (a.astype(jnp.float32) + b.astype(jnp.float32)).astype(jnp.bfloat16)
+
+    own.wait()
+
+    def vec_step(step):
+        begin(vec_copies(step, vec_now, vec_got, vsend, vrecv, at))
+
+    def vec_sum(step):
+        copies = vec_copies(step, vec_now, vec_got, vsend, vrecv, at)
+        arrive(copies)
+        total = vec_now[step]
+        for k in range(len(copies)):
+            total = total + vec_got[step + k]
+        if step < 3:
+            vec_now[step + 1] = total
+            vec_step(step + 1)
+        else:
+            vec_out[...] = total
+
+    vec_step(0)
+    for t in range(2):
+        begin(core(t))
+
+    def body(i, _):
+        @pl.when(i + 2 < NP)
+        def _():
+            begin(core(i + 2))
+
+        @pl.when(i < NP)
+        def _():
+            arrive(core(i))
+            for a in range(Y):
+                for b in range(X):
+                    local[c, a, b, :, i] = add(local[c, a, b, :, i], got_core[i, a, b])
+            begin(two(i))
+
+        @pl.when(jnp.logical_and(i >= 1, i < NP + 1))
+        def _():
+            t = i - 1
+            arrive(two(t))
+            for b in range(X):
+                local[c, y, b, 0:2, t] = add(local[c, y, b, 0:2, t], got_two[t, 0, b])
+                local[c, b, x, 2:4, t] = add(local[c, b, x, 2:4, t], got_two[t, 1, b])
+            begin(one(t))
+
+        @pl.when(jnp.logical_and(i >= 2, i < NP + 2))
+        def _():
+            t = i - 2
+            arrive(one(t))
+            for b in range(2):
+                local[c, y, x, 2 * b : 2 * b + 2, t] = add(local[c, y, x, 2 * b : 2 * b + 2, t], got_one[t, b])
+            begin(along(t))
+
+        @pl.when(i >= 3)
+        def _():
+            t = i - 3
+            arrive(along(t))
+            total = local[c, y, x, z, t].astype(jnp.float32)
+            for k in range(Z - 1):
+                total = total + got_z[t, k].astype(jnp.float32)
+            out[t] = total
+
+        for step in range(4):
+            @pl.when(i == 2 * step)
+            def _():
+                vec_sum(step)
+
+        return 0
+
+    lax.fori_loop(0, NP + 3, body, 0)
+
+    def done(t, _):
+        for copy in core(t) + two(t) + one(t) + along(t):
+            copy.wait_send()
+        return 0
+
+    lax.fori_loop(0, NP, done, 0)
+    for step in range(4):
+        for copy in vec_copies(step, vec_now, vec_got, vsend, vrecv, at):
+            copy.wait_send()
+
+
+def scatter_all(local, vec_local):
+    return pl.pallas_call(
+        scatter_kernel,
+        out_shape=(
+            jax.ShapeDtypeStruct((NP,) + PIECE, jnp.float32),
+            jax.ShapeDtypeStruct(vec_local.shape, jnp.float32),
+        ),
+        in_specs=[pl.BlockSpec(memory_space=pl.ANY), pl.BlockSpec(memory_space=pltpu.VMEM)],
+        out_specs=(pl.BlockSpec(memory_space=pltpu.VMEM), pl.BlockSpec(memory_space=pltpu.VMEM)),
+        scratch_shapes=[
+            pltpu.VMEM((C, Y, X, Z, NP) + PIECE, jnp.bfloat16),
+            pltpu.VMEM((NP, Y, X, Z) + PIECE, jnp.bfloat16),
+            pltpu.VMEM((NP, 2, 2, 2) + PIECE, jnp.bfloat16),
+            pltpu.VMEM((NP, 2, 2) + PIECE, jnp.bfloat16),
+            pltpu.VMEM((NP, Z - 1) + PIECE, jnp.bfloat16),
+            pltpu.VMEM((4,) + vec_local.shape, jnp.float32),
+            pltpu.VMEM((6,) + vec_local.shape, jnp.float32),
+            pltpu.SemaphoreType.DMA,
+            pltpu.SemaphoreType.DMA((NP, 8)),
+            pltpu.SemaphoreType.DMA((NP, 8)),
+            pltpu.SemaphoreType.DMA((6,)),
+            pltpu.SemaphoreType.DMA((6,)),
+        ],
+        compiler_params=pltpu.CompilerParams(
+            collective_id=1, has_side_effects=True, vmem_limit_bytes=56 << 20
+        ),
+        name="scatter_all",
+    )(local, vec_local)
+
+
+def to_pieces(weight):
+    if weight.shape[1] == D and weight.shape[0] != D // (Z * Y * X * C):
+        return weight.reshape(2, 48, 2, 384).transpose(0, 2, 1, 3).reshape(4, 48, 384)
+    rows, cols = weight.shape
+    return weight.reshape(rows, cols // 768, 2, 384).transpose(1, 2, 0, 3).reshape(cols // 768, 48, 384)
+
+
+def from_pieces(pieces, down):
+    if down:
+        return pieces.reshape(2, 2, 48, 384).transpose(0, 2, 1, 3).reshape(96, 768)
+    count = pieces.shape[0]
+    return pieces.reshape(count, 2, 24, 384).transpose(2, 0, 1, 3).reshape(24, count * 768)
+
+
+def whole_of(full, lo, hi):
+    count = hi - lo
+    part = full[:, :, :, :, lo:hi].reshape(C, Y, X, Z, count, 2, 24, 384)
+    return part.transpose(3, 1, 0, 2, 6, 4, 5, 7).reshape(768, count * 768)
+
+
+def whole_down(full):
+    part = full[:, :, :, :, 8:12].reshape(C, Y, X, Z, 2, 2, 48, 384)
+    return part.transpose(3, 1, 0, 2, 4, 6, 5, 7).reshape(3072, 768)
+
+
+def split_of(grad):
+    count = grad.shape[1] // 768
+    part = grad.reshape(Z, Y, C, X, 24, count, 2, 384)
+    return part.transpose(2, 1, 3, 0, 5, 6, 4, 7).reshape(C, Y, X, Z, count, 48, 384)
+
+
+def split_down(grad):
+    part = grad.reshape(Z, Y, C, X, 2, 48, 2, 384)
+    return part.transpose(2, 1, 3, 0, 4, 6, 5, 7).reshape(C, Y, X, Z, 4, 48, 384)
+
+REACH = 256
+
+
+def swap_blk(value):
+    return lax.ppermute(value, "blk", [(0, 1), (1, 0)])
+
+
+def on_device_fast(
+    tokens,
+    segments,
+    cotangent,
+    qkv_weight,
+    proj_weight,
+    up_weight,
+    down_weight,
+    vec_params,
+    qkv_velocity,
+    proj_velocity,
+    up_velocity,
+    down_velocity,
+    vec_velocity,
+    qkv_average,
+    proj_average,
+    up_average,
+    down_average,
+    vec_average,
+):
+    rows, block = (tokens.shape[0], tokens.shape[1])
+    length = segments.shape[1]
+    total_tokens = rows * lax.axis_size("dp") * length
+    rate = 0.05 / math.sqrt(total_tokens)
+    position = lax.axis_index("blk")
+    shard = lax.axis_index("dp") * lax.axis_size("blk") + position
+    masters = [w.astype(jnp.bfloat16) for w in (qkv_weight, proj_weight, up_weight, down_weight)]
+    unit = jnp.concatenate([to_pieces(w) for w in masters], axis=0)
+    vec_placed = lax.dynamic_update_slice(
+        jnp.zeros((16, D), jnp.bfloat16), vec_params.astype(jnp.bfloat16), (0, shard * vec_params.shape[1])
+    )
+    full, vec_low = gather_all(unit, vec_placed)
+    w_query, w_proj, w_up = whole_of(full, 0, 3), whole_of(full, 3, 4), whole_of(full, 4, 8)
+    w_down = whole_down(full)
+    vec = vec_low.astype(jnp.float32)
+    bias_up = vec[8:12].reshape(-1)
+    seg_query = lax.dynamic_slice_in_dim(segments, position * block, block, 1)
+    inputs = tokens.astype(jnp.float32)
+    a_one = layer_norm(inputs, vec[0], vec[1]).astype(jnp.bfloat16)
+    zero_bias = jnp.zeros_like(vec[2])
+    pre = jnp.dot(a_one, w_query, preferred_element_type=jnp.float32) + jnp.concatenate(
+        [vec[2], zero_bias, vec[3]]
+    )
+    qkv = pre.astype(jnp.bfloat16)
+    query = qkv[..., :D].reshape(rows, block, HEADS, HEAD_DIM)
+    key_value = qkv[..., D:]
+    halo = swap_blk(lax.dynamic_slice_in_dim(key_value, (1 - position) * REACH, REACH, 1))
+    near = jnp.where(
+        position == 0,
+        jnp.concatenate([key_value, halo], axis=1),
+        jnp.concatenate([halo, key_value], axis=1),
+    )
+    seg_near = lax.dynamic_slice_in_dim(segments, position * REACH, block + REACH, 1)
+    count = near.shape[1]
+    keys = near[..., :D].reshape(rows, count, HEADS, HEAD_DIM)
+    values = near[..., D:].reshape(rows, count, HEADS, HEAD_DIM)
+    scores, allowed = scores_of(query, keys, seg_query, seg_near)
+    scores = jnp.where(allowed, scores, -1e30)
+    new_top = jnp.max(scores, axis=-1)
+    weights = jnp.where(allowed, jnp.exp(scores - new_top[..., None]), 0.0)
+    denoms = jnp.sum(weights, axis=-1)
+    added = jnp.einsum(
+        "ghqk,gkhd->gqhd", weights.astype(jnp.bfloat16), values, preferred_element_type=jnp.float32
+    )
+    mixed = (added / jnp.transpose(denoms, (0, 2, 1))[..., None]).reshape(rows, block, D)
+    mixed_low = mixed.astype(jnp.bfloat16)
+    second = inputs + jnp.dot(mixed_low, w_proj, preferred_element_type=jnp.float32) + vec[4]
+    second_norm, norm_two_back = jax.vjp(layer_norm, second, vec[5], vec[6])
+    a_two = second_norm.astype(jnp.bfloat16)
+    hidden = jnp.dot(a_two, w_up, preferred_element_type=jnp.float32) + bias_up
+    act_value, gelu_back = jax.vjp(gelu_exact, hidden)
+    act = act_value.astype(jnp.bfloat16)
+    result = second + jnp.dot(act, w_down, preferred_element_type=jnp.float32) + vec[7]
+    output = result.astype(jnp.bfloat16)
+    out_grad = cotangent.astype(jnp.float32)
+    grad_down = contract_tokens(act, cotangent).astype(jnp.bfloat16)
+    bias_down_grad = jnp.sum(out_grad, axis=(0, 1))
+    act_grad = times_transpose(cotangent, w_down)
+    hidden_grad = gelu_back(act_grad)[0].astype(jnp.bfloat16)
+    bias_up_grad = jnp.sum(hidden_grad.astype(jnp.float32), axis=(0, 1))
+    grad_up = contract_tokens(a_two, hidden_grad).astype(jnp.bfloat16)
+    a_two_grad = times_transpose(hidden_grad, w_up)
+    second_part, gain_two_grad, shift_two_grad = norm_two_back(a_two_grad)
+    second_grad = out_grad + second_part
+    attn_grad = second_grad.astype(jnp.bfloat16)
+    bias_proj_grad = jnp.sum(attn_grad.astype(jnp.float32), axis=(0, 1))
+    grad_proj = contract_tokens(mixed_low, attn_grad).astype(jnp.bfloat16)
+    mixed_grad = (
+        times_transpose(attn_grad, w_proj)
+        .astype(jnp.bfloat16)
+        .reshape(rows, block, HEADS, HEAD_DIM)
+    )
+    query_grad, kv_terms = attend_back(query, near, mixed_grad, seg_query, seg_near, rows)
+    away = swap_blk(
+        lax.dynamic_slice_in_dim(kv_terms, (1 - position) * block, REACH, 1).astype(jnp.bfloat16)
+    ).astype(jnp.float32)
+    kv_own = lax.dynamic_slice_in_dim(kv_terms, position * REACH, block, 1)
+    padded = jnp.where(
+        position == 0,
+        jnp.pad(away, ((0, 0), (block - REACH, 0), (0, 0))),
+        jnp.pad(away, ((0, 0), (0, block - REACH), (0, 0))),
+    )
+    kv_grad = kv_own + padded
+    qkv_grad_low = jnp.concatenate([query_grad, kv_grad], axis=-1).astype(jnp.bfloat16)
+    qkv_sums = jnp.sum(qkv_grad_low.astype(jnp.float32), axis=(0, 1))
+    grad_query = contract_tokens(a_one, qkv_grad_low).astype(jnp.bfloat16)
+    a_one_grad = times_transpose(qkv_grad_low, w_query)
+    norm_one_back = jax.vjp(layer_norm, inputs, vec[0], vec[1])[1]
+    first_part, gain_one_grad, shift_one_grad = norm_one_back(a_one_grad)
+    tokens_grad = (second_grad + first_part).astype(jnp.bfloat16)
+    vec_local = jnp.concatenate(
+        [
+            jnp.stack(
+                [
+                    gain_one_grad,
+                    shift_one_grad,
+                    qkv_sums[:D],
+                    qkv_sums[2 * D :],
+                    bias_proj_grad,
+                    gain_two_grad,
+                    shift_two_grad,
+                    bias_down_grad,
+                ]
+            ),
+            bias_up_grad.reshape(4, D),
+            jnp.zeros((4, D), jnp.float32),
+        ],
+        axis=0,
+    )
+    local = jnp.concatenate(
+        [split_of(grad_query), split_of(grad_proj), split_of(grad_up), split_down(grad_down)], axis=4
+    )
+    pieces, vec_sum = scatter_all(local, vec_local)
+    query_share = from_pieces(pieces[0:3], False)
+    proj_share = from_pieces(pieces[3:4], False)
+    up_share = from_pieces(pieces[4:8], False)
+    down_share = from_pieces(pieces[8:12], True)
+    vec_share = lax.dynamic_slice(
+        vec_sum, (0, shard * vec_params.shape[1]), vec_params.shape
+    )
+    qkv_new = update(qkv_weight, query_share, qkv_velocity, qkv_average, rate)
+    proj_new = update(proj_weight, proj_share, proj_velocity, proj_average, rate)
+    up_new = update(up_weight, up_share, up_velocity, up_average, rate)
+    down_new = update(down_weight, down_share, down_velocity, down_average, rate)
+    vec_new = update(vec_params, vec_share, vec_velocity, vec_average, rate)
+    return (
+        output,
+        tokens_grad,
+        query_share,
+        proj_share,
+        up_share,
+        down_share,
+        vec_share,
+        qkv_new[0],
+        proj_new[0],
+        up_new[0],
+        down_new[0],
+        vec_new[0],
+        qkv_new[1],
+        proj_new[1],
+        up_new[1],
+        down_new[1],
+        vec_new[1],
+        qkv_new[2],
+        proj_new[2],
+        up_new[2],
+        down_new[2],
+        vec_new[2],
+        qkv_new[0].astype(jnp.bfloat16),
+        proj_new[0].astype(jnp.bfloat16),
+        up_new[0].astype(jnp.bfloat16),
+        down_new[0].astype(jnp.bfloat16),
+        vec_new[0].astype(jnp.bfloat16),
+    )
+
+
 def solution(mesh):
+    fits = mesh.shape["dp"] == Z * Y * C and mesh.shape["blk"] == X
     return jax.shard_map(
-        on_device,
+        on_device_fast if fits else on_device,
         mesh=mesh,
         in_specs=(
             P("dp", "blk", None),

time: 992 us -> 470 us (0.47)
  waiting for transfers between devices: 624 us -> 0.01 us
  Pallas kernels: 0 us -> 160 us
  blocking collectives: 111 us -> 0 us
  local copies, waits for them, and re-layouts: 23 us -> 128 us
  matrix products: 148 us -> 116 us
  between operations: 15.1 us -> 2.29 us
  other arithmetic: 66.1 us -> 54.5 us
    reduce_scatter x5 -> x0, waiting for transfers between devices: 449 us -> none  [the longest x1 134 us: on_device(): lax.psum_scatter(grad_down, ('dp', 'blk'), scatter_dimension=0, tiled=True)]
    all_gather x5 -> x0, waiting for transfers between devices: 175 us -> none  [the longest x1 64.3 us: on_device(): lax.all_gather(down_weight.astype(jnp.bfloat16), ('dp', 'blk'), axis=0, t...]
    pallas_call x0 -> x2, Pallas kernels: none -> 160 us  [the longest x1 82.2 us: gather_all(): pl.pallas_call(gather_kernel, out_shape=(jax.ShapeDtypeStruct((C, Y, X, Z...]
    reshape x1 -> x25, local copies, waits for them, and re-layouts: 0.01 us -> 89 us  [the longest x6 32.1 us: split_of(): part = grad.reshape(Z, Y, C, X, 24, count, 2, 384)]
    all_gather x1 -> x0, blocking collectives: 70.8 us -> none  [on_device(): lax.all_gather(vec_params.astype(jnp.bfloat16), ('dp', 'blk'), axis=1, ti...]
    unnamed x1 -> x0, blocking collectives: 40.5 us -> none
    reduce_sum x4 -> x3, other arithmetic: 19.6 us -> 3.74 us  [the longest x1 3.04 us: on_device_fast(): bias_down_grad = jnp.sum(out_grad, axis=(0, 1))]
    dot_general x6 -> x5, matrix products: 56.3 us -> 42.5 us  [the longest x1 20.4 us: on_device_fast(): hidden = jnp.dot(a_two, w_up, preferred_element_type=jnp.float32) + bias_up]
  transfers between devices with their start and end apart: 10 -> 2, of which waited for: 9 -> 0; matrix products, arithmetic and copies ran while one was open for 12% -> 22% of each run, Pallas kernels for 0% -> 0%
where the time goes in v1:
time: 470 us; the launch traced here: 463 us
  Pallas kernels  160 us (34%)
  local copies, waits for them, and re-layouts  128 us (27%)
  matrix products  116 us (25%)
  other arithmetic  54.5 us (12%)
    pallas_call x1, Pallas kernels, gather_all(): pl.pallas_call(gather_kernel, out_shape=(jax.ShapeDtypeStruct((C, Y, X, Z...  82.2 us
    pallas_call x1, Pallas kernels, scatter_all(): pl.pallas_call(scatter_kernel, out_shape=(jax.ShapeDtypeStruct((NP,) + PI...  78.1 us
    reshape x6, local copies, waits for them, and re-layouts, split_of(): part = grad.reshape(Z, Y, C, X, 24, count, 2, 384)  32.1 us
    dot_general x1, matrix products, on_device_fast(): hidden = jnp.dot(a_two, w_up, preferred_element_type=jnp.float32) + bias_up  20.4 us
    reshape x2, local copies, waits for them, and re-layouts, whole_of(): return part.transpose(3, 1, 0, 2, 6, 4, 5, 7).reshape(768, count * 768)  15.7 us
    reshape x2, local copies, waits for them, and re-layouts, split_down(): part = grad.reshape(Z, Y, C, X, 2, 48, 2, 384)  15.6 us
    dot_general x4, matrix products, contract_tokens(): lax.dot_general(left.reshape(-1, left.shape[-1]), right.reshape(-1, right...  15.3 us
    dot_general x1, matrix products, attend_back(): jnp.einsum('gqhd,gkhd->ghqk', grad_out, values, preferred_element_type=jn...  15.2 us
  transfers between devices with their start and end apart: 2, of which 0 were waited for; matrix products, arithmetic and copies ran while one was open for 22% of the time, Pallas kernels for 0%

profile of v1, /device:TPU:0, one launch (start us, length us, event | category | flops | bytes accessed | tf_op | source)
XLA Modules:
  0.0 463.4 jit_solution(1558168079109063129)
XLA Ops:
  6.7 82.2 %gather_all.1 = (bf16[2,2,2,4,12,48,384]{6,5,4,3,2,1,0:T(8,128)(2,1)}, bf16[16,768]{1,0:T(8,128)(2,1)}) custom-call(bf16[12,48,384]{2,1,0:T(8,128)(2,1)} %pad_maximum_fusion.4.unit, bf16[16,768]{1,0:T(8,128)(2,1)} %copy-done.45), custom_call_target="tpu_custom_call" | custom-call | tf_op jit(solution)/shard_map/gather_all/pallas_call | solution.py:392
  103.4 4.4 fusion.24
  118.6 8.7 %fusion.81 = (bf16[2,2,2,4,4,48,384]{6,5,4,3,2,1,0:T(8,128)(2,1)}, bf16[2,2,2,4,4,48,384]{6,5,4,3,2,1,0:T(8,128)(2,1)}) fusion(bf16[2,2,2,4,12,48,384]{6,5,4,3,2,1,0:T(8,128)(2,1)} %get-tuple-element.32), kind=kLoop, calls=%fused_computation.170 | loop fusion | bytes 18874368 | tf_op jit(solution)/shard_map/slice | solution.py:590
  127.3 9.2 %copy.91 = bf16[2,2,2,4,4,2,24,384]{7,5,4,6,2,0,1,3:T(2,128)(2,1)} copy(bf16[2,2,2,4,4,2,24,384]{7,6,5,4,3,2,1,0:T(8,128)(2,1)} %bitcast.204) | data formatting | bytes 9437184 | tf_op jit(solution)/shard_map/reshape | solution.py:585
  136.5 11.5 %reshape.702 = bf16[768,3072]{1,0:T(8,128)(2,1)} reshape(bf16[4,2,2,2,24,4,2,384]{7,6,5,4,3,2,1,0:T(2,128)(2,1)} %bitcast.201) | data formatting | bytes 9437184 | tf_op jit(solution)/shard_map/reshape | solution.py:586
  148.0 9.5 %copy.75 = bf16[2,2,2,4,2,2,48,384]{7,5,6,4,2,0,1,3:T(2,128)(2,1)} copy(bf16[2,2,2,4,2,2,48,384]{7,6,5,4,3,2,1,0:T(8,128)(2,1)} %bitcast.203) | data formatting | bytes 9437184 | tf_op jit(solution)/shard_map/reshape | solution.py:590
  157.5 5.3 %copy.86 = bf16[384,8,2,384]{3,1,2,0:T(8,128)(2,1)} copy(bf16[384,8,2,384]{3,2,1,0:T(2,128)(2,1)} %bitcast.202) | data formatting | bytes 9437184
  167.1 13.3 %fusion.72 = (f32[12,512]{1,0:T(8,128)}, f32[12,512]{1,0:T(8,128)}, f32[12,512,768]{2,1,0:T(8,128)}) fusion(pred[512,768]{1,0:T(8,128)(4,1)S(1)} %broadcast_compare_fusion, bf16[512,12,64]{0,2,1:T(8,128)(2,1)S(1)} %bitcast.212, bf16[768,12,64]{0,2,1:T(8,128)(2,1)S(1)} %bitcast.223), kind=kOutput, calls=%fused_computation.163 | convolution fusion | flops 632285952 | bytes 21282816 | tf_op jit(solution)/shard_map/sub | solution.py:670
  180.5 9.5 %fusion.42 = bf16[1,512,12,64]{1,3,2,0:T(8,128)(2,1)S(1)} fusion(bf16[768,12,64]{0,2,1:T(8,128)(2,1)S(1)} %bitcast.225, f32[12,512,768]{2,1,0:T(8,128)} %get-tuple-element.81, pred[512,768]{1,0:T(8,128)(4,1)S(1)} %broadcast_compare_fusion, f32[512,12]{0,1:T(8,128)} %bitcast.250), kind=kOutput, calls=%fused_computation.85 | convolution fusion | flops 609484800 | bytes 21258240 | tf_op jit(solution)/shard_map/ghqk,gkhd->gqhd/dot_general | solution.py:672
  191.4 20.4 %multiply_convert_fusion.1 = (bf16[512,3072]{1,0:T(8,128)(2,1)}, f32[512,3072]{1,0:T(8,128)S(1)}, f32[512,3072]{1,0:T(8,128)}) fusion(f32[3072]{0:T(1024)S(1)} %copy-done.61, bf16[768,3072]{1,0:T(8,128)(2,1)} %reshape.702, f32[1,512,768]{2,1,0:T(8,128)S(1)} %get-tuple-element.83, f32[768]{0:T(1024)S(1)} %copy-done.66, f32[768]{0:T(1024)S(1)} %copy-done.60, ...), kind=kOutput, calls=%fused_computation.30 | convolution fusion | flops 2521694208 | bytes 22042624 | tf_op jit(solution)/shard_map/dot_general | solution.py:680
  211.9 7.5 %convert_reduce_fusion = (f32[3072]{0:T(1024)}, bf16[512,3072]{1,0:T(8,128)(2,1)S(1)}) fusion(f32[512,3072]{1,0:T(8,128)S(1)} %get-tuple-element.70, bf16[3072,768]{1,0:T(8,128)(2,1)S(1)} %bitcast.218, bf16[1,512,768]{2,1,0:T(8,128)(2,1)S(1)} %copy-done.17, f32[512,3072]{1,0:T(8,128)} %get-tuple-element.84, f32[3072]{0:T(1024)S(1)} %copy-done.61), kind=kOutput, calls=%fused_computation.29 | convolution fusion | flops 2442654720 | bytes 21258240 | tf_op jit(solution)/shard_map/dot_general | solution.py:36
  229.0 15.2 %multiply_reduce_fusion = (f32[12,512]{1,0:T(8,128)S(1)}, f32[12,512,768]{2,1,0:T(8,128)}) fusion(f32[12,512,768]{2,1,0:T(8,128)} %get-tuple-element.81, f32[12,512]{1,0:T(8,128)S(1)} %copy-done.57, bf16[512,12,64]{0,2,1:T(8,128)(2,1)S(1)} %bitcast.238, bf16[768,12,64]{0,2,1:T(8,128)(2,1)S(1)} %bitcast.226), kind=kOutput, calls=%fused_computation.2 | convolution fusion | flops 618129408 | bytes 39763968 | tf_op jit(solution)/shard_map/gqhd,gkhd->ghqk/dot_general | solution.py:66
  244.2 9.0 %fusion.3 = f32[12,64,768]{2,1,0:T(8,128)} fusion(bf16[512,12,64]{0,2,1:T(8,128)(2,1)S(1)} %bitcast.239, f32[12,512,768]{2,1,0:T(8,128)} %get-tuple-element.81, f32[12,512]{1,0:T(8,128)S(1)} %copy-done.57), kind=kOutput, calls=%fused_computation.11 | convolution fusion | flops 613416960 | bytes 22044672 | tf_op jit(solution)/shard_map/ghqk,gqhd->gkhd/dot_general | solution.py:75
  253.2 12.6 %multiply_convert_fusion = bf16[12,512,768]{2,1,0:T(8,128)(2,1)S(1)} fusion(f32[12,512,768]{2,1,0:T(8,128)} %get-tuple-element.87, f32[12,512]{1,0:T(8,128)S(1)} %get-tuple-element.86, f32[12,512,768]{2,1,0:T(8,128)} %get-tuple-element.81, f32[12,512]{1,0:T(8,128)S(1)} %copy-done.57), kind=kLoop, calls=%fused_computation.1 | loop fusion | flops 18874368 | bytes 47235072 | tf_op jit(solution)/shard_map/convert_element_type | solution.py:68
  271.5 4.8 %convolution_convert_fusion.1 = bf16[768,3072]{1,0:T(8,128)(2,1)} fusion(bf16[512,3072]{1,0:T(8,128)(2,1)S(1)} %copy-done.70, f32[1,512,768]{2,1,0:T(8,128)S(1)} %copy-done.8, f32[768]{0:T(1024)S(1)} %copy-done.67, f32[768]{0:T(1024)S(1)} %copy-done.60, f32[512]{0:T(512)S(1)} %fusion.58, f32[512]{0:T(512)S(1)} %broadcast_multiply_fusion), kind=kOutput, calls=%fused_computation.49 | convolution fusion | flops 2420244480 | bytes 9447424 | tf_op jit(solution)/shard_map/dot_general | solution.py:27
  282.7 4.5 convolution_convert_fusion
  287.2 10.1 %reshape.716 = bf16[4,2,2,2,2,48,2,384]{7,6,5,4,3,2,1,0:T(2,128)(2,1)} reshape(bf16[3072,768]{1,0:T(8,128)(2,1)} %convolution_convert_fusion) | data formatting | bytes 9437184 | tf_op jit(solution)/shard_map/reshape | solution.py:601
  297.3 5.5 %copy.80 = bf16[4,2,2,2,2,48,2,384]{7,5,6,4,0,3,1,2:T(8,128)(2,1)} copy(bf16[4,2,2,2,2,48,2,384]{7,6,5,4,3,2,1,0:T(2,128)(2,1)} %reshape.716) | data formatting | bytes 9437184 | tf_op jit(solution)/shard_map/reshape | solution.py:601
  302.8 11.6 %reshape.714 = bf16[4,2,2,2,24,4,2,384]{7,6,5,4,3,2,1,0:T(2,128)(2,1)} reshape(bf16[768,3072]{1,0:T(8,128)(2,1)} %convolution_convert_fusion.1) | data formatting | bytes 9437184 | tf_op jit(solution)/shard_map/reshape | solution.py:596
  314.4 5.6 %copy.79 = bf16[4,2,2,2,24,4,2,384]{7,4,6,5,0,3,1,2:T(8,128)(2,1)} copy(bf16[4,2,2,2,24,4,2,384]{7,6,5,4,3,2,1,0:T(2,128)(2,1)} %reshape.714) | data formatting | bytes 9437184 | tf_op jit(solution)/shard_map/reshape | solution.py:596
  325.8 7.2 %fusion.46 = bf16[1,512,768]{2,1,0:T(8,128)(2,1)} fusion(f32[1,512,768]{2,1,0:T(8,128)} %copy-done.7, bf16[512,3072]{1,0:T(8,128)(2,1)} %get-tuple-element.69, bf16[3072,768]{1,0:T(8,128)(2,1)} %bitcast.215, f32[768]{0:T(1024)S(1)} %copy-done.65), kind=kOutput, calls=%fused_computation.92 | convolution fusion | flops 2417098752 | bytes 10226688 | tf_op jit(solution)/shard_map/dot_general | solution.py:683
  349.7 7.8 %reshape.710 = bf16[4,2,2,2,24,3,2,384]{7,6,5,4,3,2,1,0:T(2,128)(2,1)} reshape(bf16[768,2304]{1,0:T(8,128)(2,1)} %convolution_convert_fusion.2) | data formatting | bytes 7077888 | tf_op jit(solution)/shard_map/reshape | solution.py:596
  361.6 9.2 %pad_maximum_fusion.local_in = bf16[2,2,2,4,12,48,384]{6,5,4,3,2,1,0:T(8,128)(2,1)} fusion(bf16[2,2,2,4,4,48,384]{6,5,4,3,2,1,0:T(8,128)(2,1)S(1)} %bitcast.199, bf16[2,2,2,4,4,48,384]{6,5,4,3,2,1,0:T(8,128)(2,1)} %bitcast.200, bf16[2,2,2,4,1,48,384]{6,5,4,3,2,1,0:T(8,128)(2,1)S(1)} %bitcast.214, bf16[2,2,2,4,3,48,384]{6,5,4,3,2,1,0:T(8,128)(2,1)S(1)} %bitcast.205), kind=kLoop, calls=%fused_computation.8 | loop fusion | flops 21233664 | bytes 28311552 | tf_op jit(solution)/shard_map/concatenate | solution.py:740
  372.1 78.1 %scatter_all.1 = (f32[12,48,384]{2,1,0:T(8,128)}, f32[16,768]{1,0:T(8,128)}) custom-call(bf16[2,2,2,4,12,48,384]{6,5,4,3,2,1,0:T(8,128)(2,1)} %pad_maximum_fusion.local_in, f32[16,768]{1,0:T(8,128)} %concatenate.72.vec_in), custom_call_target="tpu_custom_call" | custom-call | tf_op jit(solution)/shard_map/scatter_all/pallas_call | solution.py:540
  (269 shorter events, 98.1 us)
Async XLA Ops:
  0.7 162.1 %copy-start = (s32[1,1024]{1,0:T(1,128)S(1)}, s32[1,1024]{1,0:T(1,128)}, u32[]{:S(2)}) copy-start(s32[1,1024]{1,0:T(1,128)} %param.19) | copy-start | bytes 12292
  90.3 13.2 %copy-start.49 = (f32[768]{0:T(1024)}, f32[768]{0:T(1024)S(1)}, u32[]{:S(2)}) copy-start(f32[768]{0:T(1024)S(1)} %get-tuple-element.48) | copy-start | bytes 9220
  101.4 6.5 %copy-start.53 = (f32[512]{0:T(512)}, f32[512]{0:T(512)S(1)}, u32[]{:S(2)}) copy-start(f32[512]{0:T(512)S(1)} %broadcast_multiply_fusion.1) | copy-start | bytes 6148
  110.3 52.8 %collective-permute-start = (bf16[1,256,1536]{2,1,0:T(8,128)(2,1)}, bf16[1,256,1536]{2,1,0:T(8,128)(2,1)}, u32[]{:S(2)}, u32[]{:S(2)}) collective-permute-start(bf16[1,256,1536]{2,1,0:T(8,128)(2,1)} %constant_dynamic-slice_fusion.2), channel_id=1, source_target_pairs={{0,1},{1,0},{2,3},{3,2},{4,5},{5,4},{6,7},{7,6},{8,9},{9,8},{10,11... | collective-permute-start | bytes 2359304 | tf_op jit(solution)/shard_map/ppermute | solution.py:608
  167.1 13.3 %copy-start.13 = (bf16[1,768,768]{1,2,0:T(8,128)(2,1)}, bf16[1,768,768]{1,2,0:T(8,128)(2,1)S(1)}, u32[]{:S(2)}) copy-start(bf16[1,768,768]{1,2,0:T(8,128)(2,1)S(1)} %copy.72) | copy-start | bytes 3538948
  167.1 13.3 %copy-start.15 = (bf16[1,768,768]{1,2,0:T(8,128)(2,1)S(1)}, bf16[1,768,768]{1,2,0:T(8,128)(2,1)}, u32[]{:S(2)}) copy-start(bf16[1,768,768]{1,2,0:T(8,128)(2,1)} %copy.70) | copy-start | bytes 3538948
  180.5 9.6 %copy-start.4 = (bf16[1,512,768]{2,1,0:T(8,128)(2,1)S(1)}, bf16[1,512,768]{2,1,0:T(8,128)(2,1)}, u32[]{:S(2)}) copy-start(bf16[1,512,768]{2,1,0:T(8,128)(2,1)} %param.18) | copy-start | bytes 2359300
  180.5 9.6 %copy-start.28 = (bf16[96,8,2,384]{3,1,2,0:T(8,128)(2,1)S(1)}, bf16[96,8,2,384]{3,1,2,0:T(8,128)(2,1)}, u32[]{:S(2)}) copy-start(bf16[96,8,2,384]{3,1,2,0:T(8,128)(2,1)} %copy.85) | copy-start | bytes 3538948
  180.5 9.6 %copy-start.68 = (f32[768]{0:T(1024)S(1)}, f32[768]{0:T(1024)}, u32[]{:S(2)}) copy-start(f32[768]{0:T(1024)} %get-tuple-element.44) | copy-start | bytes 9220
  180.5 10.9 %copy-start.60 = (f32[768]{0:T(1024)S(1)}, f32[768]{0:T(1024)}, u32[]{:S(2)}) copy-start(f32[768]{0:T(1024)} %get-tuple-element.43) | copy-start | bytes 9220
  180.5 10.9 %copy-start.61 = (f32[3072]{0:T(1024)S(1)}, f32[3072]{0:T(1024)}, u32[]{:S(2)}) copy-start(f32[3072]{0:T(1024)} %add.228) | copy-start | bytes 36868
  180.5 10.9 %copy-start.66 = (f32[768]{0:T(1024)S(1)}, f32[768]{0:T(1024)}, u32[]{:S(2)}) copy-start(f32[768]{0:T(1024)} %get-tuple-element.42) | copy-start | bytes 9220
  190.1 21.8 %slice-start.2 = ((s8[4718592]{0:T(1024)(128)(4,1)}), s8[4194304]{0:T(1024)(128)(4,1)S(1)}, s32[]{:S(2)}) async-start(s8[4718592]{0:T(1024)(128)(4,1)} %bitcast.216), calls=%async_computation.2 | async-start | bytes 8388608
  190.1 29.4 %slice-start.4 = ((s8[4718592]{0:T(1024)(128)(4,1)}), s8[4194304]{0:T(1024)(128)(4,1)S(1)}, s32[]{:S(2)}) async-start(s8[4718592]{0:T(1024)(128)(4,1)} %bitcast.219), calls=%async_computation.4 | async-start | bytes 8388608
  191.0 31.9 %copy-start.7 = (f32[1,512,768]{2,1,0:T(8,128)}, f32[1,512,768]{2,1,0:T(8,128)S(1)}, u32[]{:S(2)}) copy-start(f32[1,512,768]{2,1,0:T(8,128)S(1)} %get-tuple-element.83) | copy-start | bytes 4718596
  191.4 20.5 %slice-start.3 = ((s8[4718592]{0:T(1024)(128)(4,1)}), s8[524288]{0:T(1024)(128)(4,1)S(1)}, s32[]{:S(2)}) async-start(s8[4718592]{0:T(1024)(128)(4,1)} %bitcast.216), calls=%async_computation.3 | async-start | bytes 1048576
  191.4 20.5 %copy-start.17 = (bf16[1,512,768]{2,1,0:T(8,128)(2,1)S(1)}, bf16[1,512,768]{2,1,0:T(8,128)(2,1)}, u32[]{:S(2)}) copy-start(bf16[1,512,768]{2,1,0:T(8,128)(2,1)} %param.20) | copy-start | bytes 2359300
  191.4 28.0 %slice-start.5 = ((s8[4718592]{0:T(1024)(128)(4,1)}), s8[524288]{0:T(1024)(128)(4,1)S(1)}, s32[]{:S(2)}) async-start(s8[4718592]{0:T(1024)(128)(4,1)} %bitcast.219), calls=%async_computation.5 | async-start | bytes 1048576
  281.9 51.0 %collective-permute-start.1 = (bf16[1,256,1536]{1,2,0:T(8,128)(2,1)}, bf16[1,256,1536]{1,2,0:T(8,128)(2,1)}, u32[]{:S(2)}, u32[]{:S(2)}) collective-permute-start(bf16[1,256,1536]{1,2,0:T(8,128)(2,1)} %fusion.41), channel_id=1, source_target_pairs={{0,1},{1,0},{2,3},{3,2},{4,5},{5,4},{6,7},{7,6},{8,9},{9,8},{10,11... | collective-permute-start | bytes 2359304 | tf_op jit(solution)/shard_map/ppermute | solution.py:608
  349.7 10.7 %copy-start.20 = (bf16[12,64,512]{2,1,0:T(8,128)(2,1)S(1)}, bf16[12,64,512]{2,1,0:T(8,128)(2,1)}, u32[]{:S(2)}) copy-start(bf16[12,64,512]{2,1,0:T(8,128)(2,1)} %multiply_convert_fusion.2) | copy-start | bytes 2359300
  349.7 11.1 %slice-start = ((s8[4718592]{0:T(1024)(128)(4,1)}), s8[524288]{0:T(1024)(128)(4,1)S(1)}, s32[]{:S(2)}) async-start(s8[4718592]{0:T(1024)(128)(4,1)} %bitcast.197), calls=%async_computation | async-start | bytes 1048576
  454.4 6.3 %copy-start.38 = (f32[24,3072]{1,0:T(8,128)S(1)}, f32[24,3072]{1,0:T(8,128)}, u32[]{:S(2)}) copy-start(f32[24,3072]{1,0:T(8,128)} %param.33) | copy-start | bytes 884740
  454.4 7.1 %copy-start.27 = (f32[12,8,2,384]{3,1,2,0:T(8,128)}, f32[12,8,2,384]{3,1,2,0:T(8,128)S(1)}, u32[]{:S(2)}) copy-start(f32[12,8,2,384]{3,1,2,0:T(8,128)S(1)} %copy.88) | copy-start | bytes 884740
  456.0 6.3 %copy-start.55 = (f32[12,24]{1,0:T(8,128)}, f32[12,24]{1,0:T(8,128)S(1)}, u32[]{:S(2)}) copy-start(f32[12,24]{1,0:T(8,128)S(1)} %get-tuple-element.50) | copy-start | bytes 3460
  (57 other events, 221.2 us)
